TPU v7x, 512 devices: a whole 4x8x8 slice. The times are simulated.
512 devices in a mesh: seq: 32 (over z, x), dp: 2 (over core), tensor: 8 (over y).
Axes of the slice: x: 4, y: 8, z: 8, core: 2. Of those that a mesh axis runs over, the one named last changes fastest.
Arguments:
- head_inputs: bfloat16 [2, 2560, 16384], P('dp', 'tensor', 'seq'), may hold values from -6 to 6
- b_proj: bfloat16 [2, 16384, 128], P('dp', 'seq'), may hold values from -0.59765625 to 0.59765625
- c_proj: bfloat16 [2, 16384, 128], P('dp', 'seq'), may hold values from -0.59765625 to 0.59765625
- dt_raw: float32 [2, 40, 16384], P('dp', 'tensor', 'seq'), may hold values from -2 to 0
- a_log: float32 [40], P('tensor'), as said below
- d_skip: float32 [40], P('tensor'), may hold values from 0.5 to 1.5
- w_out: bfloat16 [2560, 2560], P('tensor', 'dp'), may hold values from -0.125 to 0.125
- out_grad: bfloat16 [2, 2560, 16384], P('dp', 'tensor', 'seq'), may hold values from -6 to 6
Outputs:
- mixed: bfloat16 [2, 2560, 16384], P('dp', 'tensor', 'seq')
- grad_inputs: bfloat16 [2, 2560, 16384], P('dp', 'tensor', 'seq')
- grad_b: bfloat16 [2, 16384, 128], P('dp', 'seq')
- grad_c: bfloat16 [2, 16384, 128], P('dp', 'seq')
- grad_dt: float32 [2, 40, 16384], P('dp', 'tensor', 'seq')
- grad_alog: float32 [40], P('tensor')
- grad_skip: float32 [40], P('tensor')
- grad_w: bfloat16 [2560, 2560], P('tensor', ('seq', 'dp'))
Inputs may be any that keep to these rules, and one draw needn't show every extreme that they name: exp(a_log) lies between 0.1 / 16384 and 0.1.
All inputs are finite; a program needn't handle non-finite values.
Results may differ from a plain program's by a relative error of at most 0.0049.
Values may be sent and summed in bfloat16 or wider, within the bound.
A program may use at most 128 MiB of HBM per device.

v0:
```python
import jax
import jax.numpy as jnp
from jax import lax
from jax.sharding import PartitionSpec as P

SPAN = 256
HIGH = lax.Precision.HIGHEST


def span_pass(carried, x_block, b_block, c_block, step_block, decay_rate):
    log_decay = step_block * decay_rate[:, None]
    cumulative = jnp.cumsum(log_decay, axis=1)
    block = cumulative.shape[1]
    indices = jnp.arange(block)
    causal = (indices[:, None] >= indices[None, :])[None, :, :]
    spread = cumulative[:, :, None] - cumulative[:, None, :]
    weights = jnp.where(causal, jnp.exp(jnp.where(causal, spread, 0.0)), 0.0)
    affinity = jnp.dot(c_block, b_block.T, precision=HIGH)
    scores = affinity[None, :, :] * weights * step_block[:, None, :]
    block_out = jnp.einsum("hps,hts->hpt", x_block, scores, precision=HIGH)
    block_out = block_out + jnp.exp(cumulative)[:, None, :] * jnp.einsum(
        "hpn,tn->hpt", carried, c_block, precision=HIGH
    )
    tail_weight = jnp.exp(cumulative[:, -1:] - cumulative) * step_block
    updated = jnp.exp(cumulative[:, -1])[:, None, None] * carried
    updated = updated + jnp.einsum(
        "hps,sn->hpn", x_block * tail_weight[:, None, :], b_block, precision=HIGH
    )
    return (updated, block_out)


def sweep(streams, b_rows, c_rows, dt_rows, alog_part, skip_part, state_in):
    head_count, head_width, length = streams.shape
    blocks = length // SPAN
    step_size = jax.nn.softplus(dt_rows)
    decay_rate = -jnp.exp(alog_part)
    x_blocks = streams.reshape(head_count, head_width, blocks, SPAN).transpose(2, 0, 1, 3)
    b_blocks = b_rows.reshape(blocks, SPAN, b_rows.shape[1])
    c_blocks = c_rows.reshape(blocks, SPAN, c_rows.shape[1])
    s_blocks = step_size.reshape(head_count, blocks, SPAN).transpose(1, 0, 2)

    def advance(carried, inputs):
        return span_pass(carried, inputs[0], inputs[1], inputs[2], inputs[3], decay_rate)

    state_end, outputs = lax.scan(advance, state_in, (x_blocks, b_blocks, c_blocks, s_blocks))
    mixed_f = outputs.transpose(1, 2, 0, 3).reshape(head_count, head_width, length)
    return (mixed_f + skip_part[:, None, None] * streams, state_end)


def per_device(head_inputs, b_proj, c_proj, dt_raw, a_log, d_skip, w_out, out_grad):
    head_count = dt_raw.shape[1]
    length = head_inputs.shape[2]
    head_width = head_inputs.shape[1] // head_count
    streams = head_inputs[0].astype(jnp.float32).reshape(head_count, head_width, length)
    b_rows = b_proj[0].astype(jnp.float32)
    c_rows = c_proj[0].astype(jnp.float32)
    dt_rows = dt_raw[0]
    decay_rate = -jnp.exp(a_log)
    step_size = jax.nn.softplus(dt_rows)
    cumulative = jnp.cumsum(step_size * decay_rate[:, None], axis=1)
    device_decay = cumulative[:, -1]
    tail_weight = jnp.exp(device_decay[:, None] - cumulative) * step_size
    local_state = jnp.einsum(
        "hpt,tn->hpn", streams * tail_weight[:, None, :], b_rows, precision=HIGH
    )
    totals = lax.all_gather(device_decay[None, :], "seq", axis=0, tiled=True)
    prefix = jnp.cumsum(totals, axis=0)
    my_index = lax.axis_index("seq")
    reached = lax.dynamic_index_in_dim(prefix, my_index, 0, keepdims=False)
    before = reached - device_decay
    shard_part = lax.all_gather(local_state[None], "seq", axis=0, tiled=True)
    row_count = shard_part.shape[0]
    indices = jnp.arange(row_count, dtype=jnp.int32)
    prefix_ends = prefix
    active = (indices < my_index)[:, None]
    weights = jnp.where(active, jnp.exp(jnp.where(active, before[None, :] - prefix_ends, 0.0)), 0.0)
    state_in = jnp.einsum("jh,jhpn->hpn", weights, shard_part, precision=HIGH)

    def local_sweep(xa, ba, ca, da, aa, sa):
        return sweep(xa, ba, ca, da, aa, sa, state_in)

    primal, pullback = jax.vjp(local_sweep, streams, b_rows, c_rows, dt_rows, a_log, d_skip)
    mixed_half = primal[0].reshape(head_count * head_width, length).astype(jnp.bfloat16)
    g_full = lax.all_gather(out_grad[0], "tensor", axis=0, tiled=True)
    cotan_sum = jnp.dot(
        lax.all_gather(w_out, "dp", axis=1, tiled=True), g_full, preferred_element_type=jnp.float32
    )
    cotan_half = cotan_sum.astype(jnp.bfloat16)
    y_cotan = (
        lax.optimization_barrier(cotan_half)
        .astype(jnp.float32)
        .reshape(head_count, head_width, length)
    )
    local_cotan = jnp.einsum(
        "hpt,tn->hpn", y_cotan * jnp.exp(cumulative)[:, None, :], c_rows, precision=HIGH
    )
    shard_part = lax.all_gather(local_cotan[None], "seq", axis=0, tiled=True)
    row_count = shard_part.shape[0]
    indices = jnp.arange(row_count, dtype=jnp.int32)
    prefix_ends = prefix
    active = (indices > my_index)[:, None]
    weights = jnp.where(
        active, jnp.exp(jnp.where(active, prefix_ends - totals - reached[None, :], 0.0)), 0.0
    )
    cotan_in = jnp.einsum("jh,jhpn->hpn", weights, shard_part, precision=HIGH)
    grads = pullback((y_cotan, cotan_in))
    w_terms = lax.dot_general(
        mixed_half, g_full, (((1,), (1,)), ((), ())), preferred_element_type=jnp.float32
    )
    grad_w = lax.psum_scatter(w_terms, ("seq", "dp"), scatter_dimension=1, tiled=True).astype(
        jnp.bfloat16
    )
    grad_b, grad_c = lax.psum((grads[1], grads[2]), "tensor")
    grad_alog, grad_skip = lax.psum((grads[4], grads[5]), ("seq", "dp"))
    grad_inputs = grads[0].reshape(head_count * head_width, length).astype(jnp.bfloat16)
    return (
        mixed_half[None],
        grad_inputs[None],
        grad_b.astype(jnp.bfloat16)[None],
        grad_c.astype(jnp.bfloat16)[None],
        grads[3][None],
        grad_alog,
        grad_skip,
        grad_w,
    )


def solution(mesh):
    in_specs = (
        P("dp", "tensor", "seq"),
        P("dp", "seq", None),
        P("dp", "seq", None),
        P("dp", "tensor", "seq"),
        P("tensor"),
        P("tensor"),
        P("tensor", "dp"),
        P("dp", "tensor", "seq"),
    )
    out_specs = (
        P("dp", "tensor", "seq"),
        P("dp", "tensor", "seq"),
        P("dp", "seq", None),
        P("dp", "seq", None),
        P("dp", "tensor", "seq"),
        P("tensor"),
        P("tensor"),
        P("tensor", ("seq", "dp")),
    )
    return jax.shard_map(
        per_device, mesh=mesh, in_specs=in_specs, out_specs=out_specs, check_vma=False
    )
```

profile of v0, /device:TPU:16, one launch (start us, length us, event | category | flops | bytes accessed | tf_op | source)
XLA Modules:
  0.0 658.8 jit_solution(519363650831749236)
XLA Ops:
  10.1 1.5 reduce-window.46
  15.4 17.3 %all-gather.9.cloned.1.call-done = bf16[320,2560]{1,0:T(8,128)(2,1)} async-done(((bf16[320,1280]{1,0:T(8,128)(2,1)}), bf16[320,2560]{1,0:T(8,128)(2,1)}) %all-gather.9.cloned.1.call-update) | async-done | bytes 1638416 | tf_op jit(solution)/shard_map/all_gather | solution.py:86
  32.7 47.4 %all-gather.13.cloned.1.call-done = bf16[1,2560,512]{2,1,0:T(8,128)(2,1)} async-done(((bf16[1,320,512]{2,1,0:T(8,128)(2,1)}), bf16[1,2560,512]{2,1,0:T(8,128)(2,1)}) %all-gather.13.cloned.1.call-update) | async-done | bytes 2621456 | tf_op jit(solution)/shard_map/all_gather | solution.py:84
  80.0 3.2 fusion.131
  87.3 76.9 %all-reduce.2 = f32[160]{0:T(256)S(1)} all-reduce(f32[160]{0:T(256)S(1)} %dynamic-update-slice), channel_id=2, replica_groups=mesh['seq'=32,'dp'=2,'tensor'=8] {'seq'}, use_global_device_ids=true, to_apply=%add.2 | all-reduce | flops 160 | bytes 1280
  167.5 7.2 %all-gather.11.cloned.1.call-done = f32[160,64,128]{2,1,0:T(8,128)} async-done(((f32[5,64,128]{2,1,0:T(8,128)}), f32[160,64,128]{2,1,0:T(8,128)}) %all-gather.11.cloned.1.call-update) | async-done | bytes 5242896 | tf_op jit(solution)/shard_map/all_gather | solution.py:71
  174.6 7.7 %fusion.125 = f32[5,1,64,128]{3,1,2,0:T(1,128)S(1)} fusion(f32[32,5,1,1]{0,2,3,1:T(1,128)S(1)} %copy.117, f32[32,5,64,128]{3,2,1,0:T(8,128)} %bitcast.487), kind=kOutput, calls=%fused_computation.159 | convolution fusion | flops 15728640 | bytes 5407360 | tf_op jit(solution)/shard_map/jh,jhpn->hpn/dot_general | solution.py:77
  185.1 23.1 %while.75 = (s32[]{:T(128)}, f32[5,64,128]{2,1,0:T(8,128)S(1)}, f32[2,5,64,256]{3,2,1,0:T(8,128)}, f32[2,5,256,256]{3,2,1,0:T(8,128)}, f32[2,128,256]{1,2,0:T(8,...) while((s32[]{:T(128)}, f32[5,64,128]{2,1,0:T(8,128)S(1)}, ...), condition=%wide.region_6.7_spmd.clone.clone, body=%wide.region_3.6_spmd.clone.clone.sunk | while | flops 607838976 | bytes 16159797 | solution.py:45
  185.2 1.5 reduce-window.60
  188.2 2.8 multiply_dynamic-update-slice_fusion.4
  192.4 2.4 fusion.212
  196.8 1.5 reduce-window.60
  199.8 2.8 multiply_dynamic-update-slice_fusion.4
  204.0 2.4 fusion.212
  208.2 1.6 copy.110
  211.3 5.4 fusion.127
  217.6 48.0 %all-gather.15.cloned.1.call-done = f32[160,64,128]{2,1,0:T(8,128)} async-done(((f32[5,64,128]{2,1,0:T(8,128)}), f32[160,64,128]{2,1,0:T(8,128)}) %all-gather.15.cloned.1.call-update) | async-done | bytes 5242896 | tf_op jit(solution)/shard_map/all_gather | solution.py:97
  265.6 7.7 %fusion.123 = f32[5,1,64,128]{3,1,2,0:T(1,128)S(1)} fusion(f32[32,5,1,1]{0,2,3,1:T(1,128)S(1)} %copy.120, f32[32,5,64,128]{3,2,1,0:T(8,128)} %bitcast.486), kind=kOutput, calls=%fused_computation.157 | convolution fusion | flops 15728640 | bytes 5407360 | tf_op jit(solution)/shard_map/jh,jhpn->hpn/dot_general | solution.py:105
  275.7 46.3 %while.76 = (s32[]{:T(128)}, f32[5]{0:T(128)S(1)}, f32[5,64,128]{2,1,0:T(8,128)S(1)}, f32[2,5,64,256]{3,2,1,0:T(8,128)}, f32[2,256,128]{2,1,0:T(8,128)}, /*index...) while((s32[]{:T(128)}, f32[5]{0:T(128)S(1)}, ...), condition=%wide.region_19.20_spmd.clone.clone, body=%wide.region_7.19_spmd.clone.clone.sunk | while | flops 1212566272 | bytes 13529267 | solution.py:45
  276.7 3.9 fusion.227
  282.7 6.3 reduce-window.62
  290.2 1.9 fusion.240
  292.4 1.8 convolution_bitcast_fusion.5
  295.4 3.0 fusion.238
  299.9 3.9 fusion.227
  305.9 6.3 reduce-window.62
  313.4 1.9 fusion.240
  315.5 1.8 convolution_bitcast_fusion.5
  318.6 3.0 fusion.238
  322.1 1.6 copy.114
  325.6 290.5 %all-reduce.8 = (f32[5]{0:T(128)}, f32[5]{0:T(128)}, bf16[320,2560]{0,1:T(8,128)(2,1)S(1)}) all-reduce(f32[5]{0:T(128)S(1)} %negate_multiply_fusion, f32[5]{0:T(128)S(1)} %reduce_sum.212, f32[320,2560]{0,1:T(8,128)} %fusion.127), channel_id=1, replica_groups=mesh['seq'=32,'dp'=2,'tensor'=8] {'seq','dp'}, use_global_device_ids=true, to_apply=%region_22.23 | all-reduce | flops 819210 | bytes 4915280 | tf_op jit(solution)/shard_map/psum | solution.py:114
  616.8 35.5 %all-reduce.9 = (bf16[512,128]{1,0:T(8,128)(2,1)}, bf16[512,128]{1,0:T(8,128)(2,1)}) all-reduce(f32[512,128]{1,0:T(8,128)S(1)} %bitcast.502, f32[512,128]{1,0:T(8,128)S(1)} %bitcast.503), channel_id=1, replica_groups=mesh['seq'=32,'dp'=2,'tensor'=8] {'tensor'}, use_global_device_ids=true, to_apply=%region_20.21 | all-reduce | flops 131072 | bytes 786432 | tf_op jit(solution)/shard_map/psum | solution.py:113
  (224 shorter events, 44.2 us)
Async XLA Ops:
  7.2 7.0 %copy-start.8 = (bf16[1,512,128]{2,1,0:T(8,128)(2,1)S(1)}, bf16[1,512,128]{2,1,0:T(8,128)(2,1)}, u32[]{:S(2)}) copy-start(bf16[1,512,128]{2,1,0:T(8,128)(2,1)} %param.13) | copy-start | bytes 393220
  7.2 25.5 %all-gather.9.cloned.1.call-start = ((), (), s32[]{:S(2)}) async-start(), calls=%async_computation | async-start | bytes 2457600 | tf_op jit(solution)/shard_map/all_gather | solution.py:86
  7.9 72.1 %all-gather.13.cloned.1.call-start = ((), (), s32[]{:S(2)}) async-start(), calls=%async_computation.2 | async-start | bytes 2949120 | tf_op jit(solution)/shard_map/all_gather | solution.py:84
  8.7 166.0 %all-gather.11.cloned.1.call-start = ((), (), s32[]{:S(2)}) async-start(), calls=%async_computation.1 | async-start | bytes 5406720 | tf_op jit(solution)/shard_map/all_gather | solution.py:71
  15.3 68.1 %copy-start.9 = (bf16[1,512,128]{2,1,0:T(8,128)(2,1)S(1)}, bf16[1,512,128]{2,1,0:T(8,128)(2,1)}, u32[]{:S(2)}) copy-start(bf16[1,512,128]{2,1,0:T(8,128)(2,1)} %param.14) | copy-start | bytes 393220
  15.3 69.2 %copy-start = (bf16[1,320,512]{2,1,0:T(8,128)(2,1)S(1)}, bf16[1,320,512]{2,1,0:T(8,128)(2,1)}, u32[]{:S(2)}) copy-start(bf16[1,320,512]{2,1,0:T(8,128)(2,1)} %param.12) | copy-start | bytes 983044
  15.3 250.2 %all-gather.15.cloned.1.call-start = ((), (), s32[]{:S(2)}) async-start(), calls=%async_computation.3 | async-start | bytes 5406720 | tf_op jit(solution)/shard_map/all_gather | solution.py:97
  83.3 83.7 %copy-start.3 = (bf16[320,512]{1,0:T(8,128)(2,1)}, bf16[320,512]{1,0:T(8,128)(2,1)S(1)}, u32[]{:S(2)}) copy-start(bf16[320,512]{1,0:T(8,128)(2,1)S(1)} %fusion.131) | copy-start | bytes 983044
  83.3 81.4 %copy-start.10 = (f32[1,5,512]{2,0,1:T(1,128)S(1)}, f32[1,5,512]{2,0,1:T(1,128)}, u32[]{:S(2)}) copy-start(f32[1,5,512]{2,0,1:T(1,128)} %param.15) | copy-start | bytes 30724
  83.3 81.6 %copy-start.11 = (f32[5]{0:T(128)S(1)}, f32[5]{0:T(128)}, u32[]{:S(2)}) copy-start(f32[5]{0:T(128)} %param.17) | copy-start | bytes 64
  191.2 3.7 copy-start.1
  194.9 0.8 copy-start.2
  202.8 3.6 copy-start.1
  206.4 0.8 copy-start.2
  211.3 5.4 copy-start.5
  322.0 1.7 copy-start.4
  322.0 2.7 copy-start.12
  323.8 293.0 %copy-start.6 = (f32[2,256,128]{2,1,0:T(8,128)S(1)}, f32[2,256,128]{2,1,0:T(8,128)}, u32[]{:S(2)}) copy-start(f32[2,256,128]{2,1,0:T(8,128)} %get-tuple-element.972) | copy-start | bytes 786436
  323.8 293.0 %copy-start.7 = (f32[2,256,128]{2,1,0:T(8,128)S(1)}, f32[2,256,128]{2,1,0:T(8,128)}, u32[]{:S(2)}) copy-start(f32[2,256,128]{2,1,0:T(8,128)} %get-tuple-element.973) | copy-start | bytes 786436
Sparse Core Ops, SparseCore 0:
  10.1 22.5 all-gather.8
  34.7 45.2 all-gather.12
  83.8 90.8 all-gather.10
  177.7 87.8 all-gather.14
where the time goes:
time: 660 us; the launch traced here: 659 us
  blocking collectives  403 us (61%)
  waiting for transfers between devices  121 us (18%)
  matrix products  63.7 us (10%)
  other arithmetic  33.6 us (5%)
  local copies, waits for them, and re-layouts  21.4 us (3%)
  between operations  15.6 us (2%)
    psum x1, blocking collectives, per_device(): grad_alog, grad_skip = lax.psum((grads[4], grads[5]), ('seq', 'dp'))  291 us
    unnamed x1, blocking collectives  76.9 us
    all_gather x1, waiting for transfers between devices, per_device(): shard_part = lax.all_gather(local_cotan[None], 'seq', axis=0, tiled=True)  48 us
    all_gather x1, waiting for transfers between devices, per_device(): g_full = lax.all_gather(out_grad[0], 'tensor', axis=0, tiled=True)  47.4 us
    psum x1, blocking collectives, per_device(): grad_b, grad_c = lax.psum((grads[1], grads[2]), 'tensor')  35.5 us
    dot_general x6, matrix products, span_pass(): block_out = jnp.einsum('hps,hts->hpt', x_block, scores, precision=HIGH)  18.5 us
    another operation x23, other arithmetic  17.6 us
    all_gather x1, waiting for transfers between devices, per_device(): lax.all_gather(w_out, 'dp', axis=1, tiled=True)  17.3 us
  transfers between devices with their start and end apart: 4, of which 4 were waited for; matrix products, arithmetic and copies ran while one was open for 9% of the time, Pallas kernels for 0%

commit v1 on v0

--- a/solution.py
+++ b/solution.py
@@ -111,7 +111,7 @@
         jnp.bfloat16
     )
     grad_b, grad_c = lax.psum((grads[1], grads[2]), "tensor")
-    grad_alog, grad_skip = lax.psum((grads[4], grads[5]), ("seq", "dp"))
+    grad_alog, grad_skip = lax.psum(lax.psum((grads[4], grads[5]), "seq"), "dp")
     grad_inputs = grads[0].reshape(head_count * head_width, length).astype(jnp.bfloat16)
     return (
         mixed_half[None],

time: 660 us -> 691 us (1.047)
  the two profiles are of different devices: /device:TPU:16 before, /device:TPU:2 now
where the time goes in v1:
time: 691 us; the launch traced here: 690 us
  blocking collectives  482 us (70%)
  waiting for transfers between devices  71.8 us (10%)
  matrix products  63.8 us (9%)
  other arithmetic  33.7 us (5%)
  local copies, waits for them, and re-layouts  22.5 us (3%)
  between operations  15.5 us (2%)
    unnamed x2, blocking collectives  366 us
    psum x2, blocking collectives, per_device(): grad_alog, grad_skip = lax.psum(lax.psum((grads[4], grads[5]), 'seq'), 'dp')  78.7 us
    all_gather x1, waiting for transfers between devices, per_device(): shard_part = lax.all_gather(local_state[None], 'seq', axis=0, tiled=True)  70.3 us
    psum x1, blocking collectives, per_device(): grad_b, grad_c = lax.psum((grads[1], grads[2]), 'tensor')  36.9 us
    dot_general x6, matrix products, span_pass(): block_out = jnp.einsum('hps,hts->hpt', x_block, scores, precision=HIGH)  18.5 us
    another operation x23, other arithmetic  17.6 us
  transfers between devices with their start and end apart: 4, of which 1 were waited for; matrix products, arithmetic and copies ran while one was open for 9% of the time, Pallas kernels for 0%

profile of v1, /device:TPU:2, one launch (start us, length us, event | category | flops | bytes accessed | tf_op | source)
XLA Modules:
  0.0 689.5 jit_solution(13781134656489730364)
XLA Ops:
  10.2 1.5 reduce-window.46
  18.2 76.9 %all-reduce.2 = f32[160]{0:T(256)S(1)} all-reduce(f32[160]{0:T(256)S(1)} %dynamic-update-slice), channel_id=2, replica_groups=mesh['seq'=32,'dp'=2,'tensor'=8] {'seq'}, use_global_device_ids=true, to_apply=%add.2 | all-reduce | flops 160 | bytes 1280
  97.9 3.3 fusion.131
  103.2 70.3 %all-gather.11.cloned.1.call-done = f32[160,64,128]{2,1,0:T(8,128)} async-done(((f32[5,64,128]{2,1,0:T(8,128)}), f32[160,64,128]{2,1,0:T(8,128)}) %all-gather.11.cloned.1.call-update) | async-done | bytes 5242896 | tf_op jit(solution)/shard_map/all_gather | solution.py:71
  173.5 7.7 %fusion.125 = f32[5,1,64,128]{3,1,2,0:T(1,128)S(1)} fusion(f32[32,5,1,1]{0,2,3,1:T(1,128)S(1)} %copy.117, f32[32,5,64,128]{3,2,1,0:T(8,128)} %bitcast.487), kind=kOutput, calls=%fused_computation.159 | convolution fusion | flops 15728640 | bytes 5407360 | tf_op jit(solution)/shard_map/jh,jhpn->hpn/dot_general | solution.py:77
  184.0 23.3 %while.75 = (s32[]{:T(128)}, f32[5,64,128]{2,1,0:T(8,128)S(1)}, f32[2,5,64,256]{3,2,1,0:T(8,128)}, f32[2,5,256,256]{3,2,1,0:T(8,128)}, f32[2,128,256]{1,2,0:T(8,...) while((s32[]{:T(128)}, f32[5,64,128]{2,1,0:T(8,128)S(1)}, ...), condition=%wide.region_6.7_spmd.clone.clone, body=%wide.region_3.6_spmd.clone.clone.sunk | while | flops 607838976 | bytes 16159797 | solution.py:45
  184.1 1.5 reduce-window.60
  187.1 2.9 multiply_dynamic-update-slice_fusion.4
  191.4 2.4 fusion.212
  195.8 1.5 reduce-window.60
  198.8 2.8 multiply_dynamic-update-slice_fusion.4
  203.1 2.4 fusion.212
  207.3 1.6 copy.110
  208.9 1.4 reshape.722
  210.3 5.3 fusion.127
  215.6 289.4 %all-reduce.10 = bf16[320,2560]{0,1:T(8,128)(2,1)} all-reduce(f32[320,2560]{0,1:T(8,128)} %fusion.127), channel_id=6, replica_groups=mesh['seq'=32,'dp'=2,'tensor'=8] {'seq','dp'}, use_global_device_ids=true, to_apply=%region_28.29.clone | all-reduce | flops 819200 | bytes 4915200
  507.3 7.7 %fusion.123 = f32[5,1,64,128]{3,1,2,0:T(1,128)S(1)} fusion(f32[32,5,1,1]{0,2,3,1:T(1,128)S(1)} %copy.120, f32[32,5,64,128]{3,2,1,0:T(8,128)} %bitcast.486), kind=kOutput, calls=%fused_computation.157 | convolution fusion | flops 15728640 | bytes 5407360 | tf_op jit(solution)/shard_map/jh,jhpn->hpn/dot_general | solution.py:105
  517.5 46.4 %while.76 = (s32[]{:T(128)}, f32[5]{0:T(128)S(1)}, f32[5,64,128]{2,1,0:T(8,128)S(1)}, f32[2,5,64,256]{3,2,1,0:T(8,128)}, f32[2,256,128]{2,1,0:T(8,128)}, /*index...) while((s32[]{:T(128)}, f32[5]{0:T(128)S(1)}, ...), condition=%wide.region_19.20_spmd.clone.clone, body=%wide.region_7.19_spmd.clone.clone.sunk | while | flops 1212566272 | bytes 13529267 | solution.py:45
  518.4 3.9 fusion.227
  524.5 6.3 reduce-window.62
  532.0 1.9 fusion.240
  534.1 1.8 convolution_bitcast_fusion.5
  537.2 3.0 fusion.238
  541.7 3.9 fusion.227
  547.7 6.3 reduce-window.62
  555.2 1.9 fusion.240
  557.4 1.8 convolution_bitcast_fusion.5
  560.4 3.0 fusion.238
  563.9 1.7 copy.114
  567.4 75.7 %all-reduce.4 = (f32[5]{0:T(128)S(1)}, f32[5]{0:T(128)S(1)}) all-reduce(f32[5]{0:T(128)S(1)} %negate_multiply_fusion, f32[5]{0:T(128)S(1)} %reduce_sum.212), channel_id=1, replica_groups=mesh['seq'=32,'dp'=2,'tensor'=8] {'seq'}, use_global_device_ids=true, to_apply=%region_22.23 | all-reduce | flops 10 | bytes 80 | tf_op jit(solution)/shard_map/psum | solution.py:114
  643.2 3.0 all-reduce.6
  646.1 36.9 %all-reduce.9 = (bf16[512,128]{1,0:T(8,128)(2,1)}, bf16[512,128]{1,0:T(8,128)(2,1)}) all-reduce(f32[512,128]{1,0:T(8,128)S(1)} %bitcast.502, f32[512,128]{1,0:T(8,128)S(1)} %bitcast.503), channel_id=1, replica_groups=mesh['seq'=32,'dp'=2,'tensor'=8] {'tensor'}, use_global_device_ids=true, to_apply=%region_20.21 | all-reduce | flops 131072 | bytes 786432 | tf_op jit(solution)/shard_map/psum | solution.py:113
  (226 shorter events, 44.0 us)
Async XLA Ops:
  7.2 8.3 %copy-start = (bf16[1,320,512]{2,1,0:T(8,128)(2,1)S(1)}, bf16[1,320,512]{2,1,0:T(8,128)(2,1)}, u32[]{:S(2)}) copy-start(bf16[1,320,512]{2,1,0:T(8,128)(2,1)} %param.12) | copy-start | bytes 983044
  7.2 7.1 %copy-start.8 = (bf16[1,512,128]{2,1,0:T(8,128)(2,1)S(1)}, bf16[1,512,128]{2,1,0:T(8,128)(2,1)}, u32[]{:S(2)}) copy-start(bf16[1,512,128]{2,1,0:T(8,128)(2,1)} %param.13) | copy-start | bytes 393220
  7.2 90.7 %all-gather.9.cloned.1.call-start = ((), (), s32[]{:S(2)}) async-start(), calls=%async_computation | async-start | bytes 2457600 | tf_op jit(solution)/shard_map/all_gather | solution.py:86
  7.9 90.0 %all-gather.13.cloned.1.call-start = ((), (), s32[]{:S(2)}) async-start(), calls=%async_computation.2 | async-start | bytes 2949120 | tf_op jit(solution)/shard_map/all_gather | solution.py:84
  8.7 164.9 %all-gather.11.cloned.1.call-start = ((), (), s32[]{:S(2)}) async-start(), calls=%async_computation.1 | async-start | bytes 5406720 | tf_op jit(solution)/shard_map/all_gather | solution.py:71
  13.1 82.4 %copy-start.9 = (bf16[1,512,128]{2,1,0:T(8,128)(2,1)S(1)}, bf16[1,512,128]{2,1,0:T(8,128)(2,1)}, u32[]{:S(2)}) copy-start(bf16[1,512,128]{2,1,0:T(8,128)(2,1)} %param.14) | copy-start | bytes 393220
  14.2 81.3 %copy-start.10 = (f32[1,5,512]{2,0,1:T(1,128)S(1)}, f32[1,5,512]{2,0,1:T(1,128)}, u32[]{:S(2)}) copy-start(f32[1,5,512]{2,0,1:T(1,128)} %param.15) | copy-start | bytes 30724
  14.2 81.5 %copy-start.11 = (f32[5]{0:T(128)S(1)}, f32[5]{0:T(128)}, u32[]{:S(2)}) copy-start(f32[5]{0:T(128)} %param.17) | copy-start | bytes 64
  15.4 491.9 %all-gather.15.cloned.1.call-start = ((), (), s32[]{:S(2)}) async-start(), calls=%async_computation.3 | async-start | bytes 5406720 | tf_op jit(solution)/shard_map/all_gather | solution.py:97
  101.2 0.7 copy-start.3
  190.2 3.7 copy-start.1
  193.9 0.8 copy-start.2
  201.8 3.6 copy-start.1
  205.5 0.8 copy-start.2
  215.6 290.8 %copy-start.5 = (f32[1,320,512]{2,1,0:T(8,128)S(1)}, f32[1,320,512]{2,1,0:T(8,128)}, u32[]{:S(2)}) copy-start(f32[1,320,512]{2,1,0:T(8,128)} %reshape.722) | copy-start | bytes 1966084
  563.8 1.8 copy-start.4
  563.9 2.7 copy-start.12
  563.9 82.3 %copy-start.6 = (f32[2,256,128]{2,1,0:T(8,128)S(1)}, f32[2,256,128]{2,1,0:T(8,128)}, u32[]{:S(2)}) copy-start(f32[2,256,128]{2,1,0:T(8,128)} %get-tuple-element.972) | copy-start | bytes 786436
  563.9 82.3 %copy-start.7 = (f32[2,256,128]{2,1,0:T(8,128)S(1)}, f32[2,256,128]{2,1,0:T(8,128)}, u32[]{:S(2)}) copy-start(f32[2,256,128]{2,1,0:T(8,128)} %get-tuple-element.973) | copy-start | bytes 786436
Sparse Core Ops, SparseCore 0:
  10.1 22.6 all-gather.8
  34.9 46.0 all-gather.12
  84.7 88.7 all-gather.10
  176.6 88.8 all-gather.14
